TPU v7x, 128 devices: a whole 4x4x4 slice. The times are simulated.
128 devices in a mesh: pool: 2 (over z_hi), grp: 8 (over x, core), tp: 8 (over z_lo, y).
Axes of the slice: x: 4, y: 4, z: 4 (z_hi: 2, z_lo: 2; z = z_hi * 2 + z_lo), core: 2. Of those that a mesh axis runs over, the one named last changes fastest.
Arguments:
- query: bfloat16 [512, 8192], P(('pool', 'grp'), 'tp'), may hold values from -6 to 6
- new_kv: bfloat16 [2, 512, 1024], P(None, ('pool', 'grp'), 'tp'), may hold values from -8 to 8
- cache: bfloat16 [2, 512, 8, 256, 128], P(None, ('pool', 'grp'), 'tp'), may hold values from -12 to 12
- lengths: int32 [512], P(('pool', 'grp')), may hold values from 1 to 256, as said below
- out_weight: bfloat16 [8192, 16384], P('tp', ('pool', 'grp')), may hold values from -0.125 to 0.125
- residual: bfloat16 [512, 16384], P('tp', ('pool', 'grp')), may hold values from -20 to 20
- norm_gain: float32 [16384], P(('pool', 'grp')), may hold values from 0.1 to 1.9
- gate_up: bfloat16 [2, 16384, 26624], P(None, ('pool', 'grp'), 'tp'), may hold values from -0.046875 to 0.046875
- down_weight: bfloat16 [26624, 16384], P('tp', ('pool', 'grp')), may hold values from -0.078125 to 0.078125
Outputs:
- layer_out: bfloat16 [512, 16384], P('tp', ('pool', 'grp'))
Inputs may be any that keep to these rules, and one draw needn't show every extreme that they name: `lengths`: every row has at least one valid position, and some row has all 256.
All inputs are finite; a program needn't handle non-finite values.
Results may differ from a plain program's by a relative error of at most 0.024.
Values may be sent and summed in bfloat16 or wider, within the bound.
A program may use at most 128 MiB of HBM per device.

v0:
```python
import jax
import jax.numpy as jnp
from jax import lax
from jax.sharding import PartitionSpec as P

D = 16384
HD = 128


def on_device(query, new_kv, cache, lengths, out_weight, residual, norm_gain, gate_up, down_weight):
    rows_here = query.shape[0]
    kv_here = cache.shape[2]
    span = cache.shape[3]
    heads_here = query.shape[1] // HD
    group = heads_here // kv_here
    scale = 1.0 / HD**0.5
    queries = query.reshape(rows_here, kv_here, group, HD)
    fresh = new_kv.reshape(2, rows_here, kv_here, HD)
    scores = (
        jnp.einsum("rkgd,rkld->rkgl", queries, cache[0], preferred_element_type=jnp.float32) * scale
    )
    own = jnp.einsum("rkgd,rkd->rkg", queries, fresh[0], preferred_element_type=jnp.float32) * scale
    valid = jnp.arange(span)[None, :] < lengths[:, None]
    scores = jnp.where(valid[:, None, None, :], scores, -jnp.inf)
    top = jnp.maximum(jnp.max(scores, axis=-1), own)
    expd = jnp.exp(scores - top[..., None])
    exp_own = jnp.exp(own - top)
    total = jnp.sum(expd, axis=-1) + exp_own
    probs = (expd / total[..., None]).astype(jnp.bfloat16)
    prob_own = (exp_own / total).astype(jnp.bfloat16)
    mixed = jnp.einsum("rkgl,rkld->rkgd", probs, cache[1], preferred_element_type=jnp.float32)
    mixed = (
        mixed
        + prob_own.astype(jnp.float32)[..., None] * fresh[1].astype(jnp.float32)[:, :, None, :]
    )
    attended = mixed.reshape(rows_here, heads_here * HD).astype(jnp.bfloat16)
    partial_value = jnp.dot(
        lax.all_gather(attended, ("pool", "grp"), axis=0, tiled=True),
        out_weight,
        preferred_element_type=jnp.float32,
    )
    hidden_state = residual.astype(jnp.float32) + lax.psum_scatter(
        partial_value.astype(jnp.bfloat16), "tp", scatter_dimension=0, tiled=True
    ).astype(jnp.float32)
    squares = lax.psum(jnp.sum(hidden_state * hidden_state, axis=1), ("pool", "grp"))
    normed = (hidden_state * lax.rsqrt(squares / D + 1e-05)[:, None] * norm_gain).astype(
        jnp.bfloat16
    )
    everyone = lax.all_gather(normed, "tp", axis=0, tiled=True)
    ff_here = gate_up.shape[2]
    local_terms = jnp.einsum(
        "rd,kdf->rkf", everyone, gate_up, preferred_element_type=jnp.float32
    ).reshape(everyone.shape[0], 2 * ff_here)
    both = lax.psum(local_terms.astype(jnp.bfloat16), ("pool", "grp")).astype(jnp.float32)
    act = (jax.nn.silu(both[:, :ff_here]) * both[:, ff_here:]).astype(jnp.bfloat16)
    partial_out = jnp.dot(act, down_weight, preferred_element_type=jnp.float32)
    down = lax.psum_scatter(
        partial_out.astype(jnp.bfloat16), "tp", scatter_dimension=0, tiled=True
    ).astype(jnp.float32)
    return (hidden_state + down).astype(jnp.bfloat16)


def solution(mesh):
    in_specs = (
        P(("pool", "grp"), "tp"),
        P(None, ("pool", "grp"), "tp"),
        P(None, ("pool", "grp"), "tp", None, None),
        P(("pool", "grp")),
        P("tp", ("pool", "grp")),
        P("tp", ("pool", "grp")),
        P(("pool", "grp")),
        P(None, ("pool", "grp"), "tp"),
        P("tp", ("pool", "grp")),
    )
    out_specs = P("tp", ("pool", "grp"))
    return jax.shard_map(
        on_device, mesh=mesh, in_specs=in_specs, out_specs=out_specs, check_vma=False
    )
```

profile of v0, /device:TPU:1, one launch (start us, length us, event | category | flops | bytes accessed | tf_op | source)
XLA Modules:
  0.0 411.8 jit_solution(9901156788616310792)
XLA Ops:
  6.5 0.0 copy-start
  6.5 0.0 all-gather.3.cloned.1.call-start
  6.5 0.9 iota_compare_fusion
  7.4 0.7 bitcast_convert_fusion
  8.1 0.8 copy.17
  9.0 0.1 fusion.16
  9.1 0.0 copy-start.1
  9.2 0.0 copy-start.3
  9.2 2.4 fusion.21
  11.5 0.2 fusion.13
  11.8 2.0 fusion.11
  13.8 0.7 copy.22
  14.5 0.0 all-gather.3.cloned.1.call-update
  14.5 0.0 reduce-scatter.3.cloned.1.call-start
  14.5 48.9 %all-gather.3.cloned.1.call-done = bf16[512,1024]{1,0:T(8,128)(2,1)} async-done(((bf16[32,1024]{1,0:T(8,128)(2,1)}), bf16[512,1024]{1,0:T(8,128)(2,1)}) %all-gather.3.cloned.1.call-update) | async-done | bytes 1048592 | tf_op jit(solution)/shard_map/all_gather | solution.py:38
  63.4 0.0 copy-done
  63.4 3.5 convolution_convert_fusion.1
  66.8 0.0 reduce-scatter.3.cloned.1.call-update
  66.9 0.0 all-gather.5.cloned.1.call-start
  66.9 32.6 %reduce-scatter.3.cloned.1.call-done = bf16[64,1024]{1,0:T(8,128)(2,1)} async-done(((bf16[512,1024]{1,0:T(8,128)(2,1)}), bf16[64,1024]{1,0:T(8,128)(2,1)}) %reduce-scatter.3.cloned.1.call-update) | async-done | bytes 131088 | tf_op jit(solution)/shard_map/reduce_scatter | solution.py:42
  99.5 0.0 copy-done.1
  99.5 1.0 multiply_reduce_fusion
  100.6 38.1 %psum.14 = f32[64]{0:T(128)S(1)} all-reduce(f32[64]{0:T(128)S(1)} %multiply_reduce_fusion), channel_id=1, replica_groups=mesh['pool'=2,'grp'=8,'tp'=8] {'pool','grp'}, use_global_device_ids=true, to_apply=%region_4.5 | all-reduce | flops 64 | bytes 512 | tf_op jit(solution)/shard_map/psum | solution.py:45
  138.7 0.0 copy-done.3
  138.7 1.7 multiply_convert_fusion
  140.3 0.0 all-gather.5.cloned.1.call-update
  140.4 0.0 all-reduce.2.cloned.1.call-start
  140.4 30.4 %all-gather.5.cloned.1.call-done = bf16[512,1024]{1,0:T(8,128)(2,1)} async-done(((bf16[64,1024]{1,0:T(8,128)(2,1)}), bf16[512,1024]{1,0:T(8,128)(2,1)}) %all-gather.5.cloned.1.call-update) | async-done | bytes 1048592 | tf_op jit(solution)/shard_map/all_gather | solution.py:49
  170.8 12.4 %convolution_convert_fusion = bf16[512,2,3328]{2,0,1:T(8,128)(2,1)} fusion(bf16[2,1024,3328]{2,1,0:T(8,128)(2,1)} %param.16, bf16[512,1024]{1,0:T(8,128)(2,1)} %all-gather.5.cloned.1.call-done), kind=kOutput, calls=%fused_computation | convolution fusion | flops 6982729728 | bytes 21495808 | tf_op jit(solution)/shard_map/rd,kdf->rkf/dot_general | solution.py:51
  183.2 10.0 %copy.14 = bf16[512,2,3328]{0,2,1:T(8,128)(2,1)} copy(bf16[512,2,3328]{2,0,1:T(8,128)(2,1)} %convolution_convert_fusion) | data formatting | bytes 13631488 | tf_op jit(solution)/shard_map/convert_element_type | solution.py:54
  193.2 0.0 all-reduce.2.cloned.1.call-update
  193.2 0.0 reduce-scatter.5.cloned.1.call-start
  193.3 161.6 %all-reduce.2.cloned.1.call-done = bf16[512,6656]{0,1:T(8,128)(2,1)} async-done(((bf16[512,6656]{0,1:T(8,128)(2,1)}), bf16[512,6656]{0,1:T(8,128)(2,1)}) %all-reduce.2.cloned.1.call-update) | async-done | bytes 6815760 | tf_op jit(solution)/shard_map/psum | solution.py:54
  354.9 4.9 %convert_element_type.76 = f32[512,6656]{0,1:T(8,128)S(1)} convert(bf16[512,6656]{0,1:T(8,128)(2,1)} %all-reduce.2.cloned.1.call-done) | non-fusion elementwise | flops 3407872 | bytes 20447232 | tf_op jit(solution)/shard_map/convert_element_type | solution.py:54
  359.8 0.0 copy-start.2
  359.8 8.0 %fusion.5 = bf16[512,1024]{1,0:T(8,128)(2,1)} fusion(bf16[3328,1024]{1,0:T(8,128)(2,1)} %param.17, f32[512,6656]{0,1:T(8,128)S(1)} %convert_element_type.76), kind=kOutput, calls=%fused_computation.8 | convolution fusion | flops 3500408832 | bytes 21495808 | tf_op jit(solution)/shard_map/dot_general | solution.py:56
  367.8 0.0 reduce-scatter.5.cloned.1.call-update
  367.8 35.8 %reduce-scatter.5.cloned.1.call-done = bf16[64,1024]{1,0:T(8,128)(2,1)} async-done(((bf16[512,1024]{1,0:T(8,128)(2,1)}), bf16[64,1024]{1,0:T(8,128)(2,1)}) %reduce-scatter.5.cloned.1.call-update) | async-done | bytes 131088 | tf_op jit(solution)/shard_map/reduce_scatter | solution.py:57
  403.6 0.0 copy-done.2
  403.7 1.6 add_convert_fusion
  (3 shorter events, 0.0 us)
Async XLA Ops:
  6.5 56.8 %copy-start = (bf16[1024,1024]{1,0:T(8,128)(2,1)S(1)}, bf16[1024,1024]{1,0:T(8,128)(2,1)}, u32[]{:S(2)}) copy-start(bf16[1024,1024]{1,0:T(8,128)(2,1)} %param.13) | copy-start | bytes 6291460
  6.5 56.8 %all-gather.3.cloned.1.call-start = ((), (), s32[]{:S(2)}) async-start(), calls=%async_computation.2 | async-start | bytes 1114112 | tf_op jit(solution)/shard_map/all_gather | solution.py:38
  9.1 90.4 %copy-start.1 = (bf16[64,1024]{1,0:T(8,128)(2,1)S(1)}, bf16[64,1024]{1,0:T(8,128)(2,1)}, u32[]{:S(2)}) copy-start(bf16[64,1024]{1,0:T(8,128)(2,1)} %param.14) | copy-start | bytes 393220
  9.2 129.5 %copy-start.3 = (f32[1024]{0:T(1024)S(1)}, f32[1024]{0:T(1024)}, u32[]{:S(2)}) copy-start(f32[1024]{0:T(1024)} %param.15) | copy-start | bytes 12292
  14.5 85.0 %reduce-scatter.3.cloned.1.call-start = ((), (), s32[]{:S(2)}) async-start(), calls=%async_computation.3 | async-start | bytes 1179648 | tf_op jit(solution)/shard_map/reduce_scatter | solution.py:42
  66.9 104.0 %all-gather.5.cloned.1.call-start = ((), (), s32[]{:S(2)}) async-start(), calls=%async_computation.4 | async-start | bytes 1179648 | tf_op jit(solution)/shard_map/all_gather | solution.py:49
  140.4 214.5 %all-reduce.2.cloned.1.call-start = ((), (), s32[]{:S(2)}) async-start(), calls=%async_computation.5 | async-start | bytes 13631488 | tf_op jit(solution)/shard_map/psum | solution.py:54
  193.2 210.4 %reduce-scatter.5.cloned.1.call-start = ((), (), s32[]{:S(2)}) async-start(), calls=%async_computation.6 | async-start | bytes 1179648 | tf_op jit(solution)/shard_map/reduce_scatter | solution.py:57
  359.8 43.9 %copy-start.2 = (bf16[64,1024]{1,0:T(8,128)(2,1)S(1)}, bf16[64,1024]{1,0:T(8,128)(2,1)}, u32[]{:S(2)}) copy-start(bf16[64,1024]{1,0:T(8,128)(2,1)} %reduce-scatter.3.cloned.1.call-done) | copy-start | bytes 393220
Sparse Core Ops, SparseCore 0:
  14.6 48.7 all-gather.2
  67.0 32.4 reduce-scatter.2
  140.5 30.3 all-gather.4
  193.4 161.4 all-reduce.1
  368.0 35.6 reduce-scatter.4
where the time goes:
time: 417 us; the launch traced here: 412 us
  waiting for transfers between devices  309 us (74%)
  blocking collectives  38.1 us (9%)
  matrix products  28.4 us (7%)
  between operations  13.2 us (3%)
  local copies, waits for them, and re-layouts  11.5 us (3%)
  other arithmetic  11 us (3%)
    psum x1, waiting for transfers between devices, on_device(): lax.psum(local_terms.astype(jnp.bfloat16), ('pool', 'grp'))  162 us
    all_gather x1, waiting for transfers between devices, on_device(): lax.all_gather(attended, ('pool', 'grp'), axis=0, tiled=True)  48.9 us
    psum x1, blocking collectives, on_device(): lax.psum(jnp.sum(hidden_state * hidden_state, axis=1), ('pool', 'grp'))  38.1 us
    reduce_scatter x1, waiting for transfers between devices, on_device(): lax.psum_scatter(partial_out.astype(jnp.bfloat16), 'tp', scatter_dimensio...  35.8 us
    reduce_scatter x1, waiting for transfers between devices, on_device(): lax.psum_scatter(partial_value.astype(jnp.bfloat16), 'tp', scatter_dimens...  32.6 us
    all_gather x1, waiting for transfers between devices, on_device(): everyone = lax.all_gather(normed, 'tp', axis=0, tiled=True)  30.4 us
    dot_general x1, matrix products, on_device(): jnp.einsum('rd,kdf->rkf', everyone, gate_up, preferred_element_type=jnp.f...  12.4 us
    convert_element_type x1, local copies, waits for them, and re-layouts, on_device(): local_terms.astype(jnp.bfloat16)  9.99 us
  transfers between devices with their start and end apart: 5, of which 5 were waited for; matrix products, arithmetic and copies ran while one was open for 0% of the time, Pallas kernels for 0%

commit v1 on v0

v1 whole, which is shorter than its diff:
```python
import jax
import jax.numpy as jnp
from jax import lax
from jax.experimental import pallas as pl
from jax.experimental.pallas import tpu as pltpu
from jax.sharding import PartitionSpec as P

MESH = pl.DeviceIdType.MESH
D = 16384
HD = 128
ROWS = 32
HEADS = 8
SPAN = 256
WIDE = 1024
FF = 3328
TILE = 256
F32 = jnp.float32
BF16 = jnp.bfloat16

A, B = (0, 1, 2), (1, 0, 2)
UNITS = (
    (0, 0, 4, A),
    (0, 4, 3, B),
    (0, 7, 3, A),
    (0, 10, 3, B),
    (1, 0, 4, B),
    (1, 4, 3, A),
    (1, 7, 3, B),
    (1, 10, 3, A),
)
NU = len(UNITS)
LAST = {half: max(u for u in range(NU) if UNITS[u][0] == half) for half in (0, 1)}


def xor_x(x, d):
    if d == 0:
        return x
    if d == 1:
        return x + 1 - 2 * lax.rem(x, 2)
    if d == 2:
        return lax.rem(x + 2, 4)
    return 3 - x


def flip(v, d):
    return 1 - v if d else v


def pick(order, k):
    index = [slice(None)] * 3
    for step in order[:k]:
        index[step] = 0
    index[order[k]] = 1
    return index


def blocks(index):
    out = [()]
    for value in index:
        choices = (0, 1) if isinstance(value, slice) else (value,)
        out = [done + (v,) for done in out for v in choices]
    return out


def within(order, k, bits):
    return tuple(bits[dim] for dim in sorted(order[k + 1 :]))


def body(*refs):
    (lens, query, fresh, residual, gain, cache, out_w, gate_up, down_w, result) = refs[:10]
    (
        qs, ks, vs, outs, kc, vc, ow, gu, dw,
        attall, pbuf, prec, pown, hid, sqall, nall, xp, act, acc, obuf, orec, oown,
    ) = refs[10:32]
    rest = refs[32:]
    parts, crecs, rec0, rec1, rec2 = (rest[i * NU : (i + 1) * NU] for i in range(5))
    (
        load, att_s, att_r, fwd_s, fwd_r, rs1_s, rs1_r, sq_s, sq_r, ag_s, ag_r,
        core_s, core_r, red_s, red_r, gat_s, gat_r, gco_s, gco_r, rs2_s, rs2_r,
    ) = rest[5 * NU :]
    recs = (rec0, rec1, rec2)

    p, g, t = lax.axis_index("pool"), lax.axis_index("grp"), lax.axis_index("tp")
    x, c = lax.div(g, 2), lax.rem(g, 2)
    zl, y = lax.div(t, 4), lax.rem(t, 4)

    def peer(dc, dx, dz):
        return (flip(p, dz), xor_x(x, dx) * 2 + flip(c, dc), t)

    def tp_of(d):
        return flip(zl, d // 4) * 4 + xor_x(y, d % 4)

    def tp_peer(d):
        return (p, g, tp_of(d))

    step_peer = (peer(0, 1, 0), peer(0, 3, 0), peer(0, 0, 1))
    others = [(dc, dx, dz) for dz in (0, 1) for dx in range(4) for dc in (0, 1)][1:]

    def remote(src, dst, send, recv, device):
        copy = pltpu.make_async_remote_copy(
            src_ref=src, dst_ref=dst, send_sem=send, recv_sem=recv, device_id=device, device_id_type=MESH
        )
        copy.start()
        return copy

    barrier = pltpu.get_barrier_semaphore()
    for other in others:
        pl.semaphore_signal(barrier, inc=1, device_id=peer(*other), device_id_type=MESH)
    for d in range(1, 8):
        pl.semaphore_signal(barrier, inc=1, device_id=tp_peer(d), device_id_type=MESH)

    loads = []

    def fetch(src, dst):
        copy = pltpu.make_async_copy(src, dst, load.at[len(loads)])
        copy.start()
        loads.append(copy)
        return copy

    caches = []
    for i in range(4):
        rows = pl.ds(i * 8, 8)
        caches.append((fetch(cache.at[0, rows, 0], kc.at[rows]), fetch(cache.at[1, rows, 0], vc.at[rows])))
    got_ow = fetch(out_w, ow)
    got_gu = [fetch(gate_up.at[k, pl.ds(i * 512, 512)], gu.at[k, pl.ds(i * 512, 512)]) for k in (0, 1) for i in (0, 1)]
    got_dw = [fetch(down_w.at[pl.ds(i * 1664, 1664)], dw.at[pl.ds(i * 1664, 1664)]) for i in (0, 1)]

    scale = 1.0 / HD**0.5
    fresh_k, fresh_v = fresh[0].astype(F32), fresh[1].astype(F32)
    for h in range(HEADS):
        qs[:, h, :] = query[:, h * HD : (h + 1) * HD].astype(F32)
        ks[:, h, :] = fresh_k
        vs[:, h, :] = fresh_v
    place = lax.broadcasted_iota(jnp.int32, (HEADS, SPAN), 1)
    for i in range(4):
        for copy in caches[i]:
            copy.wait()
        rows = range(i * 8, i * 8 + 8)
        scores, own = [], []
        for r in rows:
            q = qs[r]
            s = lax.dot_general(q.astype(BF16), kc[r], (((1,), (1,)), ((), ())), preferred_element_type=F32)
            scores.append(jnp.where(place < lens[r], s * scale, -jnp.inf))
            own.append(jnp.sum(q * ks[r], axis=1, keepdims=True) * scale)
        scores, own = jnp.concatenate(scores, axis=0), jnp.concatenate(own, axis=0)
        top = jnp.maximum(jnp.max(scores, axis=1, keepdims=True), own)
        expd, exp_own = jnp.exp(scores - top), jnp.exp(own - top)
        total = jnp.sum(expd, axis=1, keepdims=True) + exp_own
        probs = (expd / total).astype(BF16).astype(F32)
        prob_own = (exp_own / total).astype(BF16).astype(F32)
        for n, r in enumerate(rows):
            part = slice(n * HEADS, (n + 1) * HEADS)
            mixed = jnp.dot(probs[part].astype(BF16), vc[r], preferred_element_type=F32)
            outs[r] = mixed + prob_own[part] * vs[r]
    mine = g + 8 * p
    for h in range(HEADS):
        attall[mine, :, h * HD : (h + 1) * HD] = outs[:, h, :].astype(BF16)

    pl.semaphore_wait(barrier, 22)
    pending = []
    direct = [(dx, dz) for dz in (1, 0) for dx in (2, 1, 3, 0)][:-1]
    for n, (dx, dz) in enumerate(direct):
        pending.append(remote(attall.at[mine], attall.at[mine], att_s.at[n], att_r.at[n], peer(0, dx, dz)))
    pending.append(remote(attall.at[mine], attall.at[mine], fwd_s.at[7], fwd_r.at[7], peer(1, 0, 0)))
    forwards = [pending[7]]
    for n in (5, 4, 6, 3, 1, 2, 0):
        dx, dz = direct[n]
        pending[n].wait_recv()
        block = flip(p, dz) * 8 + xor_x(x, dx) * 2 + c
        forwards.append(remote(attall.at[block], attall.at[block], fwd_s.at[n], fwd_r.at[n], peer(1, 0, 0)))
    for copy in forwards:
        copy.wait_recv()
    pending += forwards[1:]

    got_ow.wait()
    half_t = lax.div(t, 2)
    for dd in (2, 3, 1, 0):
        j = flip(lax.div(half_t, 2), dd // 2) * 2 + flip(lax.rem(half_t, 2), dd % 2)
        rows = jnp.concatenate([attall[4 * j + i] for i in range(4)], axis=0)
        for n in range(WIDE // TILE):
            cols = slice(n * TILE, (n + 1) * TILE)
            prod = jnp.dot(rows, ow[:, cols], preferred_element_type=F32)
            for i in range(2):
                pbuf[2 * j + i, :, cols] = prod[i * 64 : (i + 1) * 64].astype(BF16)
                if dd == 0:
                    pown[i, :, cols] = prod[i * 64 : (i + 1) * 64]
        for d in (2 * dd, 2 * dd + 1):
            if d:
                pending.append(
                    remote(pbuf.at[tp_of(d)], prec.at[d - 1], rs1_s.at[d - 1], rs1_r.at[d - 1], tp_peer(d))
                )
    sums = pending[-7:]
    for copy in sums:
        copy.wait_recv()
    mine_t = lax.rem(t, 2)
    squares = []
    for n in range(4):
        cols = slice(n * TILE, (n + 1) * TILE)
        total = residual[:, cols].astype(F32) + pown[mine_t, :, cols]
        for d in range(7):
            total = total + prec[d, :, cols].astype(F32)
        hid[:, cols] = total
        squares.append(jnp.sum(total * total, axis=1, keepdims=True))
    square = squares[0] + squares[1] + squares[2] + squares[3]

    wide = jnp.broadcast_to(square, (64, 128))
    sqall[0] = jnp.concatenate([wide, wide], axis=0).T[:8]
    exchanged = []
    for n, other in enumerate(others):
        exchanged.append(remote(sqall.at[0], sqall.at[n + 1], sq_s.at[n], sq_r.at[n], peer(*other)))
    for copy in exchanged:
        copy.wait_recv()
    pending += exchanged
    total = sqall[0]
    for n in range(15):
        total = total + sqall[n + 1]
    factor = lax.rsqrt(total / D + 1e-05)
    factor = jnp.broadcast_to(factor[:1], (128, 128)).T[:64]
    for n in range(WIDE // 128):
        cols = slice(n * 128, (n + 1) * 128)
        normed = (hid[:, cols] * factor * gain[:, cols]).astype(BF16)
        for i in range(4):
            nall[i, :, cols] = normed[i * 16 : (i + 1) * 16]

    gathers = [None]
    for d in (1, 3, 2, 4, 5, 7, 6):
        gathers.append(
            remote(nall.at[pl.ds(0, 4)], nall.at[pl.ds(4 * d, 4)], ag_s.at[d - 1], ag_r.at[d - 1], tp_peer(d))
        )
    pending += gathers[1:]

    def owner(ic, i1, i3, iz):
        return flip(c, ic) * 8 + xor_x(x, i1 ^ (3 * i3)) * 2 + flip(p, iz)

    rels = [(ic, i1, i3, iz) for ic in (0, 1) for i1 in (0, 1) for i3 in (0, 1) for iz in (0, 1)]

    def arrange(half):
        for copy in gathers[1:4] if half == 0 else gathers[4:]:
            copy.wait_recv()
        for n, rel in enumerate(rels):
            xp[half, n] = nall[half * 16 + owner(*rel)]

    def multiply(u):
        half, first, tiles, _ = UNITS[u]
        if u == 0:
            for copy in got_gu:
                copy.wait()
        if first == 0:
            arrange(half)
        width = tiles * TILE
        for k in (0, 1):

            def tile(n, carry, k=k):
                src = pl.ds(pl.multiple_of((first + n) * TILE, TILE), TILE)
                dst = pl.ds(pl.multiple_of(k * width + n * TILE, TILE), TILE)
                rows = xp[half].reshape(256, WIDE)
                prod = jnp.dot(rows, gu[k, :, src], preferred_element_type=F32).astype(BF16)
                parts[u][:, :, :, :, :, dst] = prod.reshape(2, 2, 2, 2, 16, TILE)
                return carry

            lax.fori_loop(0, tiles, tile, 0)
        core_out[u] = remote(parts[u].at[1], crecs[u], core_s.at[u], core_r.at[u], peer(1, 0, 0))

    core_out, red_out, gat_out, gco_out = {}, {}, {}, {}

    def summed(u, k, bits, cols):
        order = UNITS[u][3]
        total = parts[u][(0,) + bits + (slice(None), cols)].astype(F32)
        total = total + crecs[u][bits + (slice(None), cols)].astype(F32)
        for j in range(k):
            total = total + recs[j][u][within(order, j, bits) + (slice(None), cols)].astype(F32)
        return total

    def reduce_step(u, k):
        _, _, tiles, order = UNITS[u]
        if k == 0:
            core_out[u].wait_recv()
        else:
            red_out[u, k - 1].wait_recv()
        index = pick(order, k)
        for bits in blocks(index):
            for n in range(2 * tiles):
                cols = slice(n * TILE, (n + 1) * TILE)
                parts[u][(0,) + bits + (slice(None), cols)] = summed(u, k, bits, cols).astype(BF16)
        red_out[u, k] = remote(
            parts[u].at[(0, *index)], recs[k][u], red_s.at[u, k], red_r.at[u, k], step_peer[order[k]]
        )

    def gather_index(u, k, bit):
        _, first, tiles, order = UNITS[u]
        index = [slice(None)] * 3
        for step in order[:k]:
            index[step] = 0
        index[order[k]] = bit
        return tuple(index) + (slice(None), pl.ds(first * TILE, tiles * TILE))

    def gather_step(u, k):
        half, first, tiles, order = UNITS[u]
        if k == 2:
            red_out[u, 2].wait_recv()
            width = tiles * TILE
            for n in range(tiles):
                gate = summed(u, 3, (0, 0, 0), slice(n * TILE, (n + 1) * TILE))
                up = summed(u, 3, (0, 0, 0), slice(width + n * TILE, width + (n + 1) * TILE))
                cols = slice((first + n) * TILE, (first + n + 1) * TILE)
                act[half, 0, 0, 0, 0, :, cols] = (gate / (1.0 + jnp.exp(-gate)) * up).astype(BF16)
        else:
            gat_out[u, k + 1].wait_recv()
        gat_out[u, k] = remote(
            act.at[(half, 0, *gather_index(u, k, 0))],
            act.at[(half, 0, *gather_index(u, k, 1))],
            gat_s.at[u, k],
            gat_r.at[u, k],
            step_peer[order[k]],
        )

    def gather_core(u):
        half, first, tiles, _ = UNITS[u]
        gat_out[u, 0].wait_recv()
        index = (slice(None),) * 4 + (pl.ds(first * TILE, tiles * TILE),)
        gco_out[u] = remote(
            act.at[(half, 0, *index)], act.at[(half, 1, *index)], gco_s.at[u], gco_r.at[u], peer(1, 0, 0)
        )

    final = []

    def down(u):
        half, first, tiles, _ = UNITS[u]
        gco_out[u].wait_recv()
        if u == 0:
            for copy in got_dw:
                copy.wait()
        width = tiles * TILE
        span = pl.ds(first * TILE, width)

        def tile(n, carry):
            cols = pl.ds(pl.multiple_of(n * TILE, TILE), TILE)
            rows = act[half, :, :, :, :, :, span].reshape(256, width)
            prod = jnp.dot(rows, dw[span, cols], preferred_element_type=F32)
            if first:
                prod = prod + acc[half, :, cols]
            acc[half, :, cols] = prod
            return carry

        lax.fori_loop(0, WIDE // TILE, tile, 0)
        if u == LAST[half]:
            for n, rel in enumerate(rels):
                block = acc[half, n * 16 : (n + 1) * 16]
                obuf[half * 16 + owner(*rel)] = block.astype(BF16)
                if half == 0:
                    oown[owner(*rel)] = block
            for d in (2, 1, 3) if half == 0 else (6, 5, 7, 4):
                final.append(
                    remote(obuf.at[pl.ds(4 * d, 4)], orec.at[d - 1], rs2_s.at[d - 1], rs2_r.at[d - 1], tp_peer(d))
                )

    actions = (
        multiply,
        lambda u: reduce_step(u, 0),
        lambda u: reduce_step(u, 1),
        lambda u: reduce_step(u, 2),
        lambda u: gather_step(u, 2),
        lambda u: gather_step(u, 1),
        lambda u: gather_step(u, 0),
        gather_core,
        down,
    )
    for wave in range(NU + len(actions) - 1):
        for u in range(NU):
            if 0 <= wave - u < len(actions):
                actions[wave - u](u)

    for copy in final:
        copy.wait_recv()
    for i in range(4):
        for n in range(WIDE // TILE):
            cols = slice(n * TILE, (n + 1) * TILE)
            total = hid[i * 16 : (i + 1) * 16, cols] + oown[i, :, cols]
            for d in range(7):
                total = total + orec[d, i, :, cols].astype(F32)
            result[i * 16 : (i + 1) * 16, cols] = total.astype(BF16)

    for copies in (core_out, red_out, gat_out, gco_out):
        pending.extend(copies.values())
    for copy in pending + final:
        copy.wait_send()


def on_device(query, new_kv, cache, lengths, out_weight, residual, norm_gain, gate_up, down_weight):
    vmem, smem, hbm = (pl.BlockSpec(memory_space=s) for s in (pltpu.VMEM, pltpu.SMEM, pl.ANY))
    dma = pltpu.SemaphoreType.DMA
    widths = [2 * TILE * tiles for _, _, tiles, _ in UNITS]
    scratch = [
        pltpu.VMEM((ROWS, HEADS, HD), F32),
        pltpu.VMEM((ROWS, HEADS, HD), F32),
        pltpu.VMEM((ROWS, HEADS, HD), F32),
        pltpu.VMEM((ROWS, HEADS, HD), F32),
        pltpu.VMEM((ROWS, SPAN, HD), BF16),
        pltpu.VMEM((ROWS, SPAN, HD), BF16),
        pltpu.VMEM((1024, WIDE), BF16),
        pltpu.VMEM((2, WIDE, FF), BF16),
        pltpu.VMEM((FF, WIDE), BF16),
        pltpu.VMEM((16, 32, 1024), BF16),
        pltpu.VMEM((8, 64, WIDE), BF16),
        pltpu.VMEM((7, 64, WIDE), BF16),
        pltpu.VMEM((2, 64, WIDE), F32),
        pltpu.VMEM((64, WIDE), F32),
        pltpu.VMEM((16, 8, 128), F32),
        pltpu.VMEM((32, 16, WIDE), BF16),
        pltpu.VMEM((2, 16, 16, WIDE), BF16),
        pltpu.VMEM((2, 2, 2, 2, 2, 16, FF), BF16),
        pltpu.VMEM((2, 256, WIDE), F32),
        pltpu.VMEM((32, 16, WIDE), BF16),
        pltpu.VMEM((7, 4, 16, WIDE), BF16),
        pltpu.VMEM((16, 16, WIDE), F32),
    ]
    scratch += [pltpu.VMEM((2, 2, 2, 2, 16, w), BF16) for w in widths]
    scratch += [pltpu.VMEM((2, 2, 2, 16, w), BF16) for w in widths]
    scratch += [pltpu.VMEM((2, 2, 16, w), BF16) for w in widths]
    scratch += [pltpu.VMEM((2, 16, w), BF16) for w in widths]
    scratch += [pltpu.VMEM((16, w), BF16) for w in widths]
    scratch += [dma((16,))]
    for shape in ((7,), (8,), (7,), (15,), (7,), (NU,), (NU, 3), (NU, 3), (NU,), (7,)):
        scratch += [dma(shape), dma(shape)]
    return pl.pallas_call(
        body,
        out_shape=jax.ShapeDtypeStruct((64, WIDE), BF16),
        in_specs=[smem, vmem, vmem, vmem, vmem, hbm, hbm, hbm, hbm],
        out_specs=vmem,
        scratch_shapes=scratch,
        compiler_params=pltpu.CompilerParams(
            collective_id=0, has_side_effects=True, vmem_limit_bytes=63 * 2**20
        ),
        cost_estimate=pl.CostEstimate(flops=11_600_000_000, bytes_accessed=27_000_000, transcendentals=1_000_000),
    )(lengths, query, new_kv, residual, norm_gain.reshape(1, WIDE), cache, out_weight, gate_up, down_weight)


def solution(mesh):
    in_specs = (
        P(("pool", "grp"), "tp"),
        P(None, ("pool", "grp"), "tp"),
        P(None, ("pool", "grp"), "tp", None, None),
        P(("pool", "grp")),
        P("tp", ("pool", "grp")),
        P("tp", ("pool", "grp")),
        P(("pool", "grp")),
        P(None, ("pool", "grp"), "tp"),
        P("tp", ("pool", "grp")),
    )
    return jax.shard_map(
        on_device, mesh=mesh, in_specs=in_specs, out_specs=P("tp", ("pool", "grp")), check_vma=False
    )
```

time: 417 us -> 153 us (0.37); the launches traced: 412 us -> 152 us
  waiting for transfers between devices: 309 us -> 0 us
  Pallas kernels: 0 us -> 151 us
  blocking collectives: 38.1 us -> 0 us
  matrix products: 28.4 us -> 0 us
  between operations: 13.2 us -> 0.01 us
  other arithmetic: 11 us -> 0 us
  local copies, waits for them, and re-layouts: 11.5 us -> 1.57 us
    psum x1 -> x0, waiting for transfers between devices: 162 us -> none  [on_device(): lax.psum(local_terms.astype(jnp.bfloat16), ('pool', 'grp'))]
    pallas_call x0 -> x1, Pallas kernels: none -> 151 us  [on_device(): pl.pallas_call(body, out_shape=jax.ShapeDtypeStruct((64, WIDE), BF16), in...]
    all_gather x2 -> x0, waiting for transfers between devices: 79.3 us -> none  [the longest x1 48.9 us: on_device(): lax.all_gather(attended, ('pool', 'grp'), axis=0, tiled=True)]
    reduce_scatter x2 -> x0, waiting for transfers between devices: 68.4 us -> none  [the longest x1 35.8 us: on_device(): lax.psum_scatter(partial_out.astype(jnp.bfloat16), 'tp', scatter_dimensio...]
    psum x1 -> x0, blocking collectives: 38.1 us -> none  [on_device(): lax.psum(jnp.sum(hidden_state * hidden_state, axis=1), ('pool', 'grp'))]
    dot_general x6 -> x0, matrix products: 28.4 us -> none  [the longest x1 12.4 us: on_device(): jnp.einsum('rd,kdf->rkf', everyone, gate_up, preferred_element_type=jnp.f...]
    convert_element_type x1 -> x0, local copies, waits for them, and re-layouts: 9.99 us -> none  [on_device(): local_terms.astype(jnp.bfloat16)]
    convert_element_type x5 -> x0, other arithmetic: 8.87 us -> none  [the longest x1 4.87 us: on_device(): lax.psum(local_terms.astype(jnp.bfloat16), ('pool', 'grp'))]
  transfers between devices with their start and end apart: 5 -> 0, of which waited for: 5 -> 0; matrix products, arithmetic and copies ran while one was open for 0% -> 0% of each run, Pallas kernels for 0% -> 0%
where the time goes in v1:
time: 153 us; the launch traced here: 152 us
  Pallas kernels  151 us (99%)
  local copies, waits for them, and re-layouts  1.57 us (1%)
    pallas_call x1, Pallas kernels, on_device(): pl.pallas_call(body, out_shape=jax.ShapeDtypeStruct((64, WIDE), BF16), in...  151 us

profile of v1, /device:TPU:1, one launch (start us, length us, event | category | flops | bytes accessed | tf_op | source)
XLA Modules:
  0.0 152.4 jit_solution(11539549743458212360)
XLA Ops:
  0.0 150.8 %shard_map.91 = bf16[64,1024]{1,0:T(8,128)(2,1)} custom-call(s32[32]{0:T(128)} %refs_0_.1, bf16[32,1024]{1,0:T(8,128)(2,1)} %refs_1_.1, bf16[2,32,128]{2,1,0:T(8,128)(2,1)} %refs_2_.1, bf16[64,1024]{1,0:T(8,128)(2,1)} %refs_3_.1, f32[1,1024]{1,0:T(1,128)} %bitcast.1, bf16[2,32,1,256,128]{4,3,2,1,0:T(8,128)(2,1)} %refs_5_.1, bf16[1024,1024]{1,0:T(8,128)(2,1)} %refs_6_.1, ...), custom_call_target="tpu_custom_call" | custom-call | flops 11600000000 | bytes 27000000 | tf_op jit(solution)/shard_map/pallas_call | solution.py:425
  150.8 1.6 %copy.11 = bf16[64,1024]{1,0:T(8,128)(2,1)} copy(bf16[64,1024]{1,0:T(8,128)(2,1)} %shard_map.91) | data formatting | bytes 262144

commit v2 on v1

v2 whole, which is shorter than its diff:
```python
import jax
import jax.numpy as jnp
from jax import lax
from jax.experimental import pallas as pl
from jax.experimental.pallas import tpu as pltpu
from jax.sharding import PartitionSpec as P

MESH = pl.DeviceIdType.MESH
D = 16384
HD = 128
ROWS = 32
HEADS = 8
SPAN = 256
WIDE = 1024
FF = 3328
TILE = 256
F32 = jnp.float32
BF16 = jnp.bfloat16

LANES = 128
A, B = (0, 1), (1, 0)
QUARTERS = 4
UNITS = (
    (0, 0, 14, A),
    (0, 14, 12, B),
    (1, 0, 14, B),
    (1, 14, 12, A),
    (2, 0, 14, A),
    (2, 14, 12, B),
    (3, 0, 14, B),
    (3, 14, 12, A),
)
NU = len(UNITS)
FIRST = {q: min(u for u in range(NU) if UNITS[u][0] == q) for q in range(QUARTERS)}


ORDER = (1, 2, 0, 3, 4, 5, 6, 7)


def xor_x(x, d):
    if d == 0:
        return x
    if d == 1:
        return x + 1 - 2 * lax.rem(x, 2)
    if d == 2:
        return lax.rem(x + 2, 4)
    return 3 - x


def flip(v, d):
    return 1 - v if d else v


def pick(order, k, bit=1):
    index = [slice(None)] * 2
    for step in order[:k]:
        index[step] = 0
    index[order[k]] = bit
    return tuple(index)


def blocks(index):
    out = [()]
    for value in index:
        choices = (0, 1) if isinstance(value, slice) else (value,)
        out = [done + (v,) for done in out for v in choices]
    return out


def pieces(first, count):
    return [(first + n, min(2, count - n)) for n in range(0, count, 2)]


def lanes(first, count):
    return slice(first * LANES, (first + count) * LANES)


def body(*refs):
    (lens, query, fresh, residual, gain, cache, out_w, gate_up, down_w, result) = refs[:10]
    (
        qs, ks, vs, outs, kc, vc, ow, gu, dw, attall, pbuf, prec, hid,
        sqall, fall, nall, xp, act, obuf, orec,
    ) = refs[10:30]
    rest = refs[30:]
    parts, crecs, rec0, rec1, rec2 = (rest[i * NU : (i + 1) * NU] for i in range(5))
    (
        load, att_s, att_r, fwd_s, fwd_r, rs1_s, rs1_r, sq_s, sq_r, fac_s, fac_r, ag_s, ag_r,
        core_s, core_r, red_s, red_r, gat_s, gat_r, gco_s, gco_r, rs2_s, rs2_r,
    ) = rest[5 * NU :]

    p, g, t = lax.axis_index("pool"), lax.axis_index("grp"), lax.axis_index("tp")
    x, c = lax.div(g, 2), lax.rem(g, 2)
    zl, y = lax.div(t, 4), lax.rem(t, 4)

    def peer(dc, dx, dz):
        return (flip(p, dz), xor_x(x, dx) * 2 + flip(c, dc), t)

    def tp_of(d):
        return flip(zl, d // 4) * 4 + xor_x(y, d % 4)

    def tp_peer(d):
        return (p, g, tp_of(d))

    step_peer = (peer(0, 1, 0), peer(0, 3, 0))
    others = [(dc, dx, dz) for dz in (0, 1) for dx in range(4) for dc in (0, 1)][1:]
    pending = []

    def remote(src, dst, send, recv, device):
        copy = pltpu.make_async_remote_copy(
            src_ref=src, dst_ref=dst, send_sem=send, recv_sem=recv, device_id=device, device_id_type=MESH
        )
        copy.start()
        pending.append(copy)
        return copy

    barrier = pltpu.get_barrier_semaphore()
    for other in others:
        pl.semaphore_signal(barrier, inc=1, device_id=peer(*other), device_id_type=MESH)
    for d in range(1, 8):
        pl.semaphore_signal(barrier, inc=1, device_id=tp_peer(d), device_id_type=MESH)

    loads = []

    def fetch(src, dst):
        copy = pltpu.make_async_copy(src, dst, load.at[len(loads)])
        copy.start()
        loads.append(copy)
        return copy

    caches = []
    for i in range(4):
        rows = pl.ds(i * 8, 8)
        caches.append((fetch(cache.at[0, rows, 0], kc.at[rows]), fetch(cache.at[1, rows, 0], vc.at[rows])))
    got_ow = fetch(out_w, ow)
    got_gu = [fetch(gate_up.at[k, pl.ds(i * 512, 512)], gu.at[k, pl.ds(i * 512, 512)]) for k in (0, 1) for i in (0, 1)]
    got_dw = [fetch(down_w.at[pl.ds(i * 1664, 1664)], dw.at[pl.ds(i * 1664, 1664)]) for i in (0, 1)]

    scale = 1.0 / HD**0.5
    fresh_k, fresh_v = fresh[0].astype(F32), fresh[1].astype(F32)
    for h in range(HEADS):
        qs[:, h, :] = query[:, h * HD : (h + 1) * HD].astype(F32)
        ks[:, h, :] = fresh_k
        vs[:, h, :] = fresh_v
    place = lax.broadcasted_iota(jnp.int32, (HEADS, SPAN), 1)
    mine = p * 4 + x

    def attend(i):
        for copy in caches[i]:
            copy.wait()
        rows = range(i * 8, i * 8 + 8)
        scores, own = [], []
        for r in rows:
            q = qs[r]
            s = lax.dot_general(q.astype(BF16), kc[r], (((1,), (1,)), ((), ())), preferred_element_type=F32)
            scores.append(jnp.where(place < lens[r], s * scale, -jnp.inf))
            own.append(jnp.sum(q * ks[r], axis=1, keepdims=True) * scale)
        scores, own = jnp.concatenate(scores, axis=0), jnp.concatenate(own, axis=0)
        top = jnp.maximum(jnp.max(scores, axis=1, keepdims=True), own)
        expd, exp_own = jnp.exp(scores - top), jnp.exp(own - top)
        total = jnp.sum(expd, axis=1, keepdims=True) + exp_own
        probs = (expd / total).astype(BF16).astype(F32)
        prob_own = (exp_own / total).astype(BF16).astype(F32)
        for n, r in enumerate(rows):
            part = slice(n * HEADS, (n + 1) * HEADS)
            mixed = jnp.dot(probs[part].astype(BF16), vc[r], preferred_element_type=F32)
            outs[r] = mixed + prob_own[part] * vs[r]

    direct = [(dx, dz) for dz in (1, 0) for dx in (2, 1, 3, 0)][:-1]
    spread = {}

    def attention(half):
        attend(2 * half)
        attend(2 * half + 1)
        for h in range(HEADS):
            attall[half, c, mine, :, h * HD : (h + 1) * HD] = outs[half * 16 : half * 16 + 16, h, :].astype(BF16)
        if half == 0:
            pl.semaphore_wait(barrier, 22)
        block = attall.at[half, c, mine]
        spread[half] = [
            remote(block, block, att_s.at[half, n], att_r.at[half, n], peer(0, *direct[n])) for n in range(7)
        ]
        spread[half].append(remote(block, block, fwd_s.at[half, 7], fwd_r.at[half, 7], peer(1, 0, 0)))

    def pass_on(half):
        forwards = [spread[half][7]]
        for n in (5, 4, 6, 3, 1, 2, 0):
            dx, dz = direct[n]
            spread[half][n].wait_recv()
            block = attall.at[half, c, flip(p, dz) * 4 + xor_x(x, dx)]
            forwards.append(remote(block, block, fwd_s.at[half, n], fwd_r.at[half, n], peer(1, 0, 0)))
        for copy in forwards:
            copy.wait_recv()

    sums = {}

    def project(q):
        rows = attall[q // 2, q % 2].reshape(128, 1024)
        for n in range(WIDE // TILE):
            cols = slice(n * TILE, (n + 1) * TILE)
            prod = jnp.dot(rows, ow[:, cols], preferred_element_type=F32)
            pbuf[q, :, :, cols] = prod.astype(BF16).reshape(8, 16, TILE)
        sums[q] = [
            remote(pbuf.at[q, tp_of(d)], prec.at[q, d - 1], rs1_s.at[q, d - 1], rs1_r.at[q, d - 1], tp_peer(d))
            for d in (6, 4, 2, 5, 7, 1, 3)
        ]

    gathers, squares = {}, {}

    def rows_of(q):
        first = q % 2 * 32 + q // 2 * 16
        return slice(first, first + 16)

    def add_up(q):
        for copy in sums[q]:
            copy.wait_recv()
        square = 0.0
        for n in range(WIDE // TILE):
            cols = slice(n * TILE, (n + 1) * TILE)
            total = residual[rows_of(q), cols].astype(F32) + pbuf[q, t, :, cols].astype(F32)
            for d in range(7):
                total = total + prec[q, d, :, cols].astype(F32)
            hid[q, :, cols] = total
            square = square + jnp.sum(total * total, axis=1, keepdims=True)
            nall[q, 0, :, cols] = (total * gain[:, cols]).astype(BF16)
        squares[q] = square
        gathers[q] = [
            remote(nall.at[q, 0], nall.at[q, d], ag_s.at[q, d - 1], ag_r.at[q, d - 1], tp_peer(d))
            for d in (6, 4, 2, 5, 7, 1, 3)
        ]

    square_copies, factor_copies = {}, {}

    def share_squares(half):
        both = [jnp.broadcast_to(squares[2 * half + e], (16, 128)) for e in (0, 1)]
        sqall[half, 0] = jnp.concatenate(both * 4, axis=0).T[:8]
        square_copies[half] = [
            remote(sqall.at[half, 0], sqall.at[half, n + 1], sq_s.at[half, n], sq_r.at[half, n], peer(*other))
            for n, other in enumerate(others)
        ]

    def share_factor(half):
        for copy in square_copies[half]:
            copy.wait_recv()
        total = sqall[half, 0]
        for n in range(15):
            total = total + sqall[half, n + 1]
        fall[half, 0] = lax.rsqrt(total / D + 1e-05)
        factor_copies[half] = [
            remote(fall.at[half, 0], fall.at[half, d], fac_s.at[half, d - 1], fac_r.at[half, d - 1], tp_peer(d))
            for d in range(1, 8)
        ]

    rels = [(ic, i1, i3) for ic in (0, 1) for i1 in (0, 1) for i3 in (0, 1)]

    def owner(ic, i1, i3):
        return flip(c, ic) * 4 + xor_x(x, i1 ^ (3 * i3))

    def arrange(q):
        for copy in gathers[q]:
            copy.wait_recv()
        for n, rel in enumerate(rels):
            xp[q, n] = nall[q, owner(*rel)]

    core_out, red_out, gat_out, gco_out = {}, {}, {}, {}
    factors, final = {}, {}

    def multiply(u):
        q, first, count, _ = UNITS[u]
        if u == 0:
            for copy in got_gu:
                copy.wait()
        if u == FIRST[q]:
            arrange(q)
        rows = xp.at[q]
        for k in (0, 1):

            def tile(src, dst, width, k=k):
                prod = jnp.dot(rows[...].reshape(128, WIDE), gu[k, :, pl.ds(src, width)], preferred_element_type=F32)
                parts[u][:, :, :, :, pl.ds(dst, width)] = prod.astype(BF16).reshape(2, 2, 2, 16, width)

            def step(n, carry, k=k, tile=tile):
                src = pl.multiple_of(first * LANES + n * TILE, LANES)
                tile(src, pl.multiple_of(k * count * LANES + n * TILE, LANES), TILE)
                return carry

            lax.fori_loop(0, count // 2, step, 0, unroll=True)
            if count % 2:
                tile((first + count - 1) * LANES, (k * count + count - 1) * LANES, LANES)
        core_out[u] = remote(parts[u].at[1], crecs[u], core_s.at[u], core_r.at[u], peer(1, 0, 0))

    def summed(u, k, bits, cols):
        order = UNITS[u][3]
        total = parts[u][(0, *bits, slice(None), cols)].astype(F32)
        total = total + crecs[u][(*bits, slice(None), cols)].astype(F32)
        if k > 0:
            total = total + rec0[u][bits[order[1]], :, cols].astype(F32)
        if k > 1:
            total = total + rec1[u][:, cols].astype(F32)
        return total

    def reduce_step(u, k):
        _, _, count, order = UNITS[u]
        if k == 0:
            core_out[u].wait_recv()
        else:
            red_out[u, k - 1].wait_recv()
        index = pick(order, k) if k < 2 else (0, 0)
        for bits in blocks(index):
            for first, n in pieces(0, 2 * count):
                cols = lanes(first, n)
                total = summed(u, k, bits, cols)
                parts[u][(0, *bits, slice(None), cols)] = total.astype(BF16)
        device = step_peer[order[k]] if k < 2 else peer(0, 0, 1)
        red_out[u, k] = remote(
            parts[u].at[(0, *index)], (rec0, rec1, rec2)[k][u], red_s.at[u, k], red_r.at[u, k], device
        )

    def factor(q):
        half = q // 2
        if half not in factors:
            for copy in factor_copies[half]:
                copy.wait_recv()
            factors[half] = jnp.broadcast_to(fall[half, owner(0, 0, 0)][:1], (128, 128)).T
        return factors[half][q % 2 * 16 : q % 2 * 16 + 16]

    def activate(u):
        q, first, count, order = UNITS[u]
        red_out[u, 2].wait_recv()
        scales = factor(q)
        for n in range(count):
            gate, up = (
                (parts[u][0, 0, 0, :, lanes(n + k * count, 1)].astype(F32) + rec2[u][:, lanes(n + k * count, 1)].astype(F32))
                * scales
                for k in (0, 1)
            )
            act[q, 0, 0, 0, :, lanes(first + n, 1)] = (gate / (1.0 + jnp.exp(-gate)) * up).astype(BF16)
        gather_step(u, 1)

    def gather_step(u, k):
        q, first, count, order = UNITS[u]
        if k == 0:
            gat_out[u, 1].wait_recv()
        cols = pl.ds(first * LANES, count * LANES)
        gat_out[u, k] = remote(
            act.at[(q, 0, *pick(order, k, 0), slice(None), cols)],
            act.at[(q, 0, *pick(order, k, 1), slice(None), cols)],
            gat_s.at[u, k],
            gat_r.at[u, k],
            step_peer[order[k]],
        )

    def gather_core(u):
        q, first, count, _ = UNITS[u]
        gat_out[u, 0].wait_recv()
        index = (slice(None),) * 3 + (pl.ds(first * LANES, count * LANES),)
        gco_out[u] = remote(
            act.at[(q, 0, *index)], act.at[(q, 1, *index)], gco_s.at[u], gco_r.at[u], peer(1, 0, 0)
        )

    def down(q):
        for u in range(NU):
            if UNITS[u][0] == q:
                gco_out[u].wait_recv()
        if q == 0:
            for copy in got_dw:
                copy.wait()

        def tile(n, carry):
            cols = pl.ds(pl.multiple_of(n * TILE, TILE), TILE)
            prod = jnp.dot(act[q].reshape(128, FF), dw[:, cols], preferred_element_type=F32).astype(BF16)
            for i, rel in enumerate(rels):
                obuf[q, owner(*rel), :, cols] = prod[i * 16 : (i + 1) * 16]
            return carry

        lax.fori_loop(0, WIDE // TILE, tile, 0, unroll=True)
        final[q] = [
            remote(obuf.at[q, d], orec.at[q, d - 1], rs2_s.at[q, d - 1], rs2_r.at[q, d - 1], tp_peer(d))
            for d in (6, 4, 2, 5, 7, 1, 3)
        ]

    def finish(q):
        for copy in final[q]:
            copy.wait_recv()
        for n in range(WIDE // TILE):
            cols = slice(n * TILE, (n + 1) * TILE)
            total = hid[q, :, cols] + obuf[q, 0, :, cols].astype(F32)
            for d in range(7):
                total = total + orec[q, d, :, cols].astype(F32)
            result[rows_of(q), cols] = total.astype(BF16)

    attention(0)
    attention(1)
    pass_on(0)
    got_ow.wait()
    project(0)
    project(1)
    pass_on(1)
    project(2)
    add_up(0)
    project(3)
    add_up(1)
    share_squares(0)
    add_up(2)
    actions = (
        multiply,
        lambda u: reduce_step(u, 0),
        lambda u: reduce_step(u, 1),
        lambda u: reduce_step(u, 2),
        activate,
        lambda u: gather_step(u, 0),
        gather_core,
    )
    for wave in range(QUARTERS + len(actions)):
        for n in ORDER:
            q = wave - n
            if 0 <= q < QUARTERS:
                if n < len(actions):
                    actions[n](2 * q)
                    actions[n](2 * q + 1)
                else:
                    down(q)
        if wave == 0:
            add_up(3)
            share_squares(1)
            share_factor(0)
        if wave == 1:
            share_factor(1)
    for q in range(QUARTERS):
        finish(q)
    for copy in pending:
        copy.wait_send()


def on_device(query, new_kv, cache, lengths, out_weight, residual, norm_gain, gate_up, down_weight):
    vmem, smem, hbm = (pl.BlockSpec(memory_space=s) for s in (pltpu.VMEM, pltpu.SMEM, pl.ANY))
    dma = pltpu.SemaphoreType.DMA
    widths = [2 * LANES * count for _, _, count, _ in UNITS]
    scratch = [
        pltpu.VMEM((ROWS, HEADS, HD), F32),
        pltpu.VMEM((ROWS, HEADS, HD), F32),
        pltpu.VMEM((ROWS, HEADS, HD), F32),
        pltpu.VMEM((ROWS, HEADS, HD), F32),
        pltpu.VMEM((ROWS, SPAN, HD), BF16),
        pltpu.VMEM((ROWS, SPAN, HD), BF16),
        pltpu.VMEM((1024, WIDE), BF16),
        pltpu.VMEM((2, WIDE, FF), BF16),
        pltpu.VMEM((FF, WIDE), BF16),
        pltpu.VMEM((2, 2, 8, 16, 1024), BF16),
        pltpu.VMEM((QUARTERS, 8, 16, WIDE), BF16),
        pltpu.VMEM((QUARTERS, 7, 16, WIDE), BF16),
        pltpu.VMEM((QUARTERS, 16, WIDE), F32),
        pltpu.VMEM((2, 16, 8, 128), F32),
        pltpu.VMEM((2, 8, 8, 128), F32),
        pltpu.VMEM((QUARTERS, 8, 16, WIDE), BF16),
        pltpu.VMEM((QUARTERS, 8, 16, WIDE), BF16),
        pltpu.VMEM((QUARTERS, 2, 2, 2, 16, FF), BF16),
        pltpu.VMEM((QUARTERS, 8, 16, WIDE), BF16),
        pltpu.VMEM((QUARTERS, 7, 16, WIDE), BF16),
    ]
    scratch += [pltpu.VMEM((2, 2, 2, 16, w), BF16) for w in widths]
    scratch += [pltpu.VMEM((2, 2, 16, w), BF16) for w in widths]
    scratch += [pltpu.VMEM((2, 16, w), BF16) for w in widths]
    scratch += [pltpu.VMEM((16, w), BF16) for w in widths]
    scratch += [pltpu.VMEM((16, w), BF16) for w in widths]
    scratch += [dma((16,))]
    for shape in (
        (2, 7), (2, 8), (4, 7), (2, 15), (2, 7), (4, 7), (NU,), (NU, 3), (NU, 2), (NU,), (4, 7),
    ):
        scratch += [dma(shape), dma(shape)]
    return pl.pallas_call(
        body,
        out_shape=jax.ShapeDtypeStruct((64, WIDE), BF16),
        in_specs=[smem, vmem, vmem, vmem, vmem, hbm, hbm, hbm, hbm],
        out_specs=vmem,
        scratch_shapes=scratch,
        compiler_params=pltpu.CompilerParams(
            collective_id=0, has_side_effects=True, vmem_limit_bytes=63 * 2**20
        ),
        cost_estimate=pl.CostEstimate(flops=11_600_000_000, bytes_accessed=27_000_000, transcendentals=1_000_000),
    )(lengths, query, new_kv, residual, norm_gain.reshape(1, WIDE), cache, out_weight, gate_up, down_weight)


def solution(mesh):
    in_specs = (
        P(("pool", "grp"), "tp"),
        P(None, ("pool", "grp"), "tp"),
        P(None, ("pool", "grp"), "tp", None, None),
        P(("pool", "grp")),
        P("tp", ("pool", "grp")),
        P("tp", ("pool", "grp")),
        P(("pool", "grp")),
        P(None, ("pool", "grp"), "tp"),
        P("tp", ("pool", "grp")),
    )
    return jax.shard_map(
        on_device, mesh=mesh, in_specs=in_specs, out_specs=P("tp", ("pool", "grp")), check_vma=False
    )
```

time: 153 us -> 105 us (0.69)
  Pallas kernels: 151 us -> 103 us
    pallas_call x1, Pallas kernels: 151 us -> 103 us  [on_device(): pl.pallas_call(body, out_shape=jax.ShapeDtypeStruct((64, WIDE), BF16), in...]
where the time goes in v2:
time: 105 us
  Pallas kernels  103 us (98%)
  local copies, waits for them, and re-layouts  1.57 us (1%)
    pallas_call x1, Pallas kernels, on_device(): pl.pallas_call(body, out_shape=jax.ShapeDtypeStruct((64, WIDE), BF16), in...  103 us

profile of v2, /device:TPU:1, one launch (start us, length us, event | category | flops | bytes accessed | tf_op | source)
XLA Modules:
  0.0 104.8 jit_solution(15256343818484142936)
XLA Ops:
  0.0 103.2 %shard_map.91 = bf16[64,1024]{1,0:T(8,128)(2,1)} custom-call(s32[32]{0:T(128)} %refs_0_.1, bf16[32,1024]{1,0:T(8,128)(2,1)} %refs_1_.1, bf16[2,32,128]{2,1,0:T(8,128)(2,1)} %refs_2_.1, bf16[64,1024]{1,0:T(8,128)(2,1)} %refs_3_.1, f32[1,1024]{1,0:T(1,128)} %bitcast.1, bf16[2,32,1,256,128]{4,3,2,1,0:T(8,128)(2,1)} %refs_5_.1, bf16[1024,1024]{1,0:T(8,128)(2,1)} %refs_6_.1, ...), custom_call_target="tpu_custom_call" | custom-call | flops 11600000000 | bytes 27000000 | tf_op jit(solution)/shard_map/pallas_call | solution.py:470
  103.3 1.6 %copy.11 = bf16[64,1024]{1,0:T(8,128)(2,1)} copy(bf16[64,1024]{1,0:T(8,128)(2,1)} %shard_map.91) | data formatting | bytes 262144

commit v3 on v2

--- a/solution.py
+++ b/solution.py
@@ -34,7 +34,14 @@
 FIRST = {q: min(u for u in range(NU) if UNITS[u][0] == q) for q in range(QUARTERS)}
 
 
-ORDER = (1, 2, 0, 3, 4, 5, 6, 7)
+ORDER = (
+    ("P", 0), ("P", 2), ("P", 1), ("S", 0), (0, 0), (0, 1), (1, 0), (1, 1), ("P", 3), ("S", 1), (0, 2), (0, 3),
+    (1, 2), (1, 3), (0, 4), (0, 5), (2, 0), (2, 1), (1, 4), (1, 5), (0, 6), (0, 7), (2, 2), (3, 0), (2, 3), (3,
+    1), (1, 6), (1, 7), (2, 5), (3, 3), ("T", 0), (2, 4), (3, 2), (4, 0), (2, 6), (3, 5), (4, 3), (4, 1), (2, 7),
+    (3, 4), (4, 2), (3, 6), (5, 1), (5, 0), ("T", 1), (3, 7), (5, 2), (4, 5), (5, 3), (4, 4), (6, 1), (6, 0), (4,
+    6), (4, 7), (6, 3), (6, 2), (5, 4), (5, 5), ("D", 0), (5, 6), (5, 7), ("D", 1), (6, 5), (6, 4), (6, 6), (6,
+    7), ("D", 2), ("D", 3), ("F", 2), ("F", 0), ("F", 1), ("F", 3),
+)
 
 
 def xor_x(x, d):
@@ -396,11 +403,7 @@
     project(1)
     pass_on(1)
     project(2)
-    add_up(0)
     project(3)
-    add_up(1)
-    share_squares(0)
-    add_up(2)
     actions = (
         multiply,
         lambda u: reduce_step(u, 0),
@@ -410,23 +413,9 @@
         lambda u: gather_step(u, 0),
         gather_core,
     )
-    for wave in range(QUARTERS + len(actions)):
-        for n in ORDER:
-            q = wave - n
-            if 0 <= q < QUARTERS:
-                if n < len(actions):
-                    actions[n](2 * q)
-                    actions[n](2 * q + 1)
-                else:
-                    down(q)
-        if wave == 0:
-            add_up(3)
-            share_squares(1)
-            share_factor(0)
-        if wave == 1:
-            share_factor(1)
-    for q in range(QUARTERS):
-        finish(q)
+    steps = {'P': add_up, 'S': share_squares, 'T': share_factor, 'D': down, 'F': finish}
+    for step, n in ORDER:
+        (actions[step] if isinstance(step, int) else steps[step])(n)
     for copy in pending:
         copy.wait_send()
 

time: 105 us -> 103 us (0.981)
  Pallas kernels: 103 us -> 101 us
    pallas_call x1, Pallas kernels: 103 us -> 101 us  [on_device(): pl.pallas_call(body, out_shape=jax.ShapeDtypeStruct((64, WIDE), BF16), in...]
where the time goes in v3:
time: 103 us
  Pallas kernels  101 us (98%)
  local copies, waits for them, and re-layouts  1.57 us (2%)
    pallas_call x1, Pallas kernels, on_device(): pl.pallas_call(body, out_shape=jax.ShapeDtypeStruct((64, WIDE), BF16), in...  101 us

profile of v3, /device:TPU:1, one launch (start us, length us, event | category | flops | bytes accessed | tf_op | source)
XLA Modules:
  0.0 102.7 jit_solution(9562905458019888172)
XLA Ops:
  0.0 101.2 %shard_map.91 = bf16[64,1024]{1,0:T(8,128)(2,1)} custom-call(s32[32]{0:T(128)} %refs_0_.1, bf16[32,1024]{1,0:T(8,128)(2,1)} %refs_1_.1, bf16[2,32,128]{2,1,0:T(8,128)(2,1)} %refs_2_.1, bf16[64,1024]{1,0:T(8,128)(2,1)} %refs_3_.1, f32[1,1024]{1,0:T(1,128)} %bitcast.1, bf16[2,32,1,256,128]{4,3,2,1,0:T(8,128)(2,1)} %refs_5_.1, bf16[1024,1024]{1,0:T(8,128)(2,1)} %refs_6_.1, ...), custom_call_target="tpu_custom_call" | custom-call | flops 11600000000 | bytes 27000000 | tf_op jit(solution)/shard_map/pallas_call | solution.py:459
  101.2 1.6 %copy.11 = bf16[64,1024]{1,0:T(8,128)(2,1)} copy(bf16[64,1024]{1,0:T(8,128)(2,1)} %shard_map.91) | data formatting | bytes 262144
